TPU v7x, 256 devices: a whole 4x4x8 slice. The times are simulated.
256 devices in a mesh: frames: 32 (over z_hi, x, core), feats: 8 (over y, z_lo).
Axes of the slice: x: 4, y: 4, z: 8 (z_hi: 4, z_lo: 2; z = z_hi * 2 + z_lo), core: 2. Of those that a mesh axis runs over, the one named last changes fastest.
Arguments:
- frames_data: bfloat16 [49152, 4096], P('frames', 'feats')
- lag_index: int32 [49152], P('frames'), may hold values from 1 to 49151, as said below
- projection: bfloat16 [4096, 64], P('feats'), may hold values from -0.09375 to 0.09375
- center_ids: int32 [256], replicated, may hold values from 0 to 49151
- nearest_prev: float32 [49152], P('frames'), may hold values from 0.5 to 2.5
Outputs:
- instant_cov: float32 [4096, 4096], P('frames', 'feats')
- lagged_cov: float32 [4096, 4096], P('frames', 'feats')
- coords: float32 [64, 49152], P(None, 'frames')
- nearest: float32 [49152], P('frames')
Inputs may be any that keep to these rules, and one draw needn't show every extreme that they name: lag_index[r] = min(r + lag[r], 49151), where each frame r has its own lag[r] of 1 to 512 (lags differ from frame to frame); it exceeds r for every frame but the last.
All inputs are finite; a program needn't handle non-finite values.
Results may differ from a plain program's by a relative error of at most 0.0003.
Values may be sent and summed in bfloat16 or wider, within the bound.
A program may use at most 128 MiB of HBM per device.

v0:
```python
import functools

import jax
import jax.numpy as jnp
from jax import lax
from jax.experimental import pallas as pl
from jax.experimental.pallas import tpu as pltpu
from jax.sharding import PartitionSpec as P

MESH = pl.DeviceIdType.MESH
F32 = jnp.float32
BF16 = jnp.bfloat16
I16 = jnp.int16

ROWS = 1536
FB = 512
LAG = 512
TOTAL = 49152
K = 64
C = 256
CH = 256
NCH = ROWS // CH
NALL = (ROWS + LAG) // CH
HF = FB // 2
LEVELS = 32767.0

OFFSETS = ((0, 0), (1, 0), (3, 0), (1, 1))
UNITS = (
    (0, 0, 0), (0, 0, 1), (1, 0, 0), (2, 0, 0), (3, 0, 0), (1, 0, 1), (2, 0, 1), (2, 1, 0),
    (2, 1, 1), (0, 3, 0), (1, 3, 0), (2, 3, 0), (0, 3, 1), (1, 3, 1), (2, 3, 1), (3, 0, 1),
)
LAG_SLOT = {0: 0, 1: 1, 3: 2}
NU = len(UNITS)
XS = 32


def dot(a, b, dims, precision=None):
    return lax.dot_general(a, b, ((dims[:1], dims[1:]), ((), ())), precision=precision, preferred_element_type=F32)


def kernel(
    x_ref, idx_ref, proj_ref, ids_ref, prev_ref,
    both_ref, coords_ref, near_ref,
    xb, lb, u, cx, s1, s1s, r1, r1s, s2, s2s, r2, r2s, zf, zfs, zs, zss, zr, zrs, es, ec, ecs, oc, ocs,
    cpart, crecv, csum, call, cen, cenr, cenall,
    ysend, yrecv, fsend, frecv, hsend, hrecv,
    cxsend, cxrecv, s1send, s1recv, s2send, s2recv, zfsend, zfrecv, zsend, zrecv, esend, erecv,
    psend, precv, gsend, grecv, nsend, nrecv, msend, mrecv,
):
    p = lax.axis_index("frames")
    q = lax.axis_index("feats")
    zh, x, c = p // 8, (p // 2) % 4, p % 2
    y, zl = q // 2, q % 2

    def at(zh_, x_, c_):
        return zh_ * 8 + x_ * 2 + c_

    xp = (at(zh, (x + 1) % 4, c), q)
    xm = (at(zh, (x + 3) % 4, c), q)
    core = (at(zh, x, 1 - c), q)

    def yto(t):
        return (p, ((y + t) % 4) * 2 + zl)

    yp, ym = yto(1), yto(3)
    zo = (p, y * 2 + 1 - zl)
    before = ((p + 31) % 32, q)

    def remote(src, dst, ss, rs, dev):
        return pltpu.make_async_remote_copy(
            src_ref=src, dst_ref=dst, send_sem=ss, recv_sem=rs, device_id=dev, device_id_type=MESH
        )

    barrier = pltpu.get_barrier_semaphore()
    peers = [core, zo, before, ((p + 1) % 32, q)]
    peers += [yto(t) for t in (1, 2, 3)]
    peers += [(at(zh, (x + t) % 4, c), q) for t in (1, 2, 3)]
    peers += [(at((zh + t) % 4, x, c), q) for t in (1, 2, 3)]
    for dev in peers:
        pl.semaphore_signal(barrier, inc=1, device_id=dev, device_id_type=MESH)
    pl.semaphore_wait(barrier, len(peers))

    sent = []

    def send(src, dst, ss, rs, dev):
        r = remote(src, dst, ss, rs, dev)
        r.start()
        sent.append((r, None))
        return r

    def send_if(cond, src, dst, ss, rs, dev):
        r = remote(src, dst, ss, rs, dev)

        @pl.when(cond)
        def _():
            r.start()

        sent.append((r, cond))
        return r

    def part(slot, h, j):
        return xb.at[slot, pl.ds(h * HF, HF), pl.ds(j * CH, CH)]

    def from_y(w, h, j):
        slot = (1, 2)[w]
        return remote(part(0, h, j), part(slot, h, j), ysend.at[w, h, j], yrecv.at[w, h, j], (ym, yp)[w])

    def to_y(w, h, j):
        if j < NCH:
            r = from_y(w, h, j)
            r.start()
            sent.append((r, None))
        else:
            r = from_y(w, h, j)

            @pl.when(c == 1)
            def _():
                r.start()

            sent.append((r, c == 1))

    def on_chip(slot, h, j):
        if j < NALL - NCH:
            k = (0, 1)[slot == 3]
            rs = (yrecv.at[0, h, NCH + j], frecv.at[h, NCH + j])[slot == 3]
            send_if(c == 1, part(slot, h, j), part(slot, h, NCH + j), hsend.at[k, h, j], rs, core)

    def forward(h, j):
        r = remote(part(1, h, j), part(3, h, j), fsend.at[h, j], frecv.at[h, j], zo)
        if j < NCH:
            from_y(0, h, j).wait_recv()
            r.start()
            sent.append((r, None))
            on_chip(1, h, j)
        else:
            @pl.when(c == 1)
            def _():
                from_y(0, h, j).wait_recv()
                r.start()

            sent.append((r, c == 1))

    def following(h):
        for j in range(NCH, NALL):
            @pl.when(c == 0)
            def _():
                from_y(0, h, j).wait_recv()

    def from_z(h, j):
        remote(part(1, h, j), part(3, h, j), fsend.at[h, j], frecv.at[h, j], zo).wait_recv()
        on_chip(3, h, j)

    for j in range(NCH):
        xb[0, :, pl.ds(j * CH, CH)] = x_ref[pl.ds(j * CH, CH), :].T
        if j == 1:
            head = send(xb.at[0, :, pl.ds(0, LAG)], xb.at[0, :, pl.ds(ROWS, LAG)], hsend.at[2, 0, 0], hrecv, before)
        if j < 3:
            to_y(0, 0, j)
            to_y(1, 0, j)

    kq = K // 4
    cpart[...] = dot(proj_ref[...], xb[0, :, 0:ROWS], (1, 0))
    crs = []
    for t in (1, 3, 2):
        rows = pl.ds(pl.multiple_of(((y + t) % 4) * kq, kq), kq)
        crs.append(send(cpart.at[rows, :], crecv.at[t], psend.at[t], precv.at[t], yto(t)))
    for j in range(3, NCH):
        to_y(0, 0, j)
        to_y(1, 0, j)
    own_rows = pl.ds(pl.multiple_of(y * kq, kq), kq)
    first = p * ROWS
    small = {}

    def coords1():
        for r in crs:
            r.wait_recv()
        csum[0] = cpart[own_rows, :] + crecv[1] + crecv[2] + crecv[3]
        small["z"] = send(csum.at[0], csum.at[1], psend.at[4], precv.at[4], zo)

    def coords2():
        small["z"].wait_recv()
        total = csum[0] + csum[1]
        call[own_rows, :] = total
        for t in (1, 3, 2):
            send(call.at[own_rows, :], call.at[own_rows, :], gsend.at[t], grecv.at[t], yto(t))
        pick = (lax.broadcasted_iota(jnp.int32, (ROWS, C), 0) + first == ids_ref[...].reshape(1, C)).astype(F32)
        cen[0] = dot(total, pick, (1, 0), lax.Precision.HIGHEST)
        small["n"] = [send(cen.at[0], cenr.at[0], nsend.at[0], nrecv.at[0], core)]

    def centers1():
        for r in small["n"]:
            r.wait_recv()
        cen[1] = cen[0] + cenr[0]
        small["n"] = [
            send(cen.at[1], cenr.at[t], nsend.at[t], nrecv.at[t], (at(zh, (x + t) % 4, c), q)) for t in (1, 2, 3)
        ]

    def centers2():
        for r in small["n"]:
            r.wait_recv()
        cen[2] = cen[1] + cenr[1] + cenr[2] + cenr[3]
        small["n"] = [
            send(cen.at[2], cenr.at[3 + t], nsend.at[3 + t], nrecv.at[3 + t], (at((zh + t) % 4, x, c), q))
            for t in (1, 2, 3)
        ]

    def centers3():
        for r in small["n"]:
            r.wait_recv()
        cenall[own_rows, :] = cen[2] + cenr[4] + cenr[5] + cenr[6]
        for t in (1, 3, 2):
            send(cenall.at[own_rows, :], cenall.at[own_rows, :], msend.at[t], mrecv.at[t], yto(t))

    def nearest():
        for t in (1, 2, 3):
            frm = pl.ds(pl.multiple_of(((y + 4 - t) % 4) * kq, kq), kq)
            remote(call.at[frm, :], call.at[frm, :], gsend.at[t], grecv.at[t], core).wait_recv()
            remote(cenall.at[frm, :], cenall.at[frm, :], msend.at[t], mrecv.at[t], core).wait_recv()
        coords = call[...]
        coords_ref[...] = coords
        centers = cenall[...]
        ones = jnp.ones((8, K), F32)
        square_y = jnp.sum(coords * coords, axis=0, keepdims=True)
        square_c = dot(centers * centers, ones, (0, 1), lax.Precision.HIGHEST)[:, 0:1]
        cross = dot(centers, coords, (0, 0), lax.Precision.HIGHEST)
        dist = (square_c + square_y - 2.0 * cross) * (1.0 / K)
        near_ref[...] = jnp.minimum(prev_ref[...].reshape(1, ROWS), jnp.min(dist, axis=0, keepdims=True))

    def gather(slot, start, size):
        at_slot = LAG_SLOT[slot]
        feats = pl.ds(start, size)

        def body(i, carry):
            base = pl.multiple_of(i * 256, 256)
            here = idx_ref[pl.ds(base, 256)].reshape(1, 256) - (first + base)
            pick = (lax.broadcasted_iota(jnp.int32, (768, 256), 0) == here).astype(F32).astype(BF16)
            lb[at_slot, feats, pl.ds(base, 256)] = dot(xb[slot, feats, pl.ds(base, 768)], pick, (1, 0)).astype(BF16)
            return carry

        lax.fori_loop(0, ROWS // 256, body, 0)

    def encode(value, out, scale_out):
        top = jnp.maximum(jnp.max(jnp.abs(value), axis=0, keepdims=True), 1e-30)
        scale_out[...] = top * (1.0 / LEVELS)
        out[...] = jnp.round(value * (LEVELS / top)).astype(jnp.int32).astype(I16)

    def decode(code, scale):
        return code[...].astype(jnp.int32).astype(F32) * scale[...]

    cxs, s1w, s2w = {}, {}, {}
    mine = pl.ds(pl.multiple_of(c * 128, 128), 128)
    other = pl.ds(pl.multiple_of((1 - c) * 128, 128), 128)

    def stage0(k):
        a, b, h = UNITS[k]
        left = xb[a, pl.ds(h * HF, HF), 0:ROWS]
        u[k, :, 0:FB] = dot(left, xb[b, :, 0:ROWS], (1, 1))
        u[k, :, FB:2 * FB] = dot(left, lb[LAG_SLOT[b]], (1, 1))
        cxs[k] = send(u.at[k, other, :], cx.at[k], cxsend.at[k], cxrecv.at[k], core)

    def slice_of(xs):
        return pl.ds(pl.multiple_of(c * 128 + xs * XS, XS), XS)

    def stage1(k):
        cxs[k].wait_recv()
        u[k, mine, :] = u[k, mine, :] + cx[k]
        encode(u[k, slice_of((x + 2) % 4), :], s1.at[k], s1s.at[k])
        out = []
        for j, dev in ((0, xp), (1, xm)):
            rows = pl.ds(j * 16, 16)
            out.append(send(s1.at[k, rows, :], r1.at[k, rows, :], s1send.at[k, j, 0], s1recv.at[k, j, 0], dev))
            out.append(send(s1s.at[k], r1s.at[k, j], s1send.at[k, j, 1], s1recv.at[k, j, 1], dev))
        s1w[k] = out

    def stage2(k):
        for r in s1w[k]:
            r.wait_recv()
        out = []
        for j, dev, xs in ((0, xp, (x + 1) % 4), (1, xm, (x + 3) % 4)):
            value = u[k, slice_of(xs), :]
            half = decode(r1.at[k, pl.ds(j * 16, 16), :], r1s.at[k, j])
            near, far = (value[0:16] + half, value[16:32]) if j == 0 else (value[0:16], value[16:32] + half)
            encode(jnp.concatenate([near, far], axis=0), s2.at[k, j], s2s.at[k, j])
            out.append(send(s2.at[k, j], r2.at[k, j], s2send.at[k, j, 0], s2recv.at[k, j, 0], dev))
            out.append(send(s2s.at[k, j], r2s.at[k, j], s2send.at[k, j, 1], s2recv.at[k, j, 1], dev))
        s2w[k] = out

    def z_owner(k):
        return (y + OFFSETS[UNITS[k][0]][0]) % 4

    def z_halves(k):
        out = []
        for j, t in ((0, 1), (1, 3)):
            cols = pl.ds(j * FB, FB)
            dev = (at((zh + t) % 4, x, c), q)
            out.append(remote(zs.at[k, :, cols], zf.at[k], zfsend.at[k, j, 0], zfrecv.at[k, 0], dev))
            out.append(remote(zss.at[k, :, cols], zfs.at[k], zfsend.at[k, j, 1], zfrecv.at[k, 1], dev))
        return out

    def z_last(k, j):
        dev = (at(z_owner(k), x, c), q)
        return (
            remote(zs.at[k], zr.at[k, j], zsend.at[k, 0], zrecv.at[k, j, 0], dev),
            remote(zss.at[k], zrs.at[k, j], zsend.at[k, 1], zrecv.at[k, j, 1], dev),
        )

    def z_place(k):
        return (zh + 4 - z_owner(k)) % 4

    def stage3(k):
        for r in s2w[k]:
            r.wait_recv()
        rows = slice_of(x)
        es[k] = u[k, rows, :] + decode(r2.at[k, 0], r2s.at[k, 0]) + decode(r2.at[k, 1], r2s.at[k, 1])

        @pl.when(z_place(k) == 2)
        def _():
            encode(es[k], zs.at[k], zss.at[k])
            for r in z_halves(k):
                r.start()

    def stage4(k):
        for j, place in ((0, 1), (1, 3)):
            @pl.when(z_place(k) == place)
            def _():
                for r in z_halves(k)[:2]:
                    r.wait_recv()
                cols = pl.ds((1 - j) * FB, FB)
                es[k, :, cols] = es[k, :, cols] + decode(zf.at[k], zfs.at[k])
                encode(es[k], zs.at[k], zss.at[k])
                for r in z_last(k, j):
                    r.start()

    def e_send(k):
        a, b, h = UNITS[k]
        rowblock = z_owner(k) * 2 + (zl + OFFSETS[a][1]) % 2
        colblock = ((y + OFFSETS[b][0]) % 4) * 2 + (zl + OFFSETS[b][1]) % 2
        owner = rowblock * 4 + h * 2 + c
        pairs = ((ec.at[k], oc.at[x]), (ecs.at[k], ocs.at[x]))
        far = [remote(src, dst, esend.at[k, i], erecv.at[i], (owner, colblock)) for i, (src, dst) in enumerate(pairs)]
        return owner, b == 0, pairs, far

    def stage5(k):
        @pl.when(z_place(k) == 0)
        def _():
            total = es[k]
            for j in range(2):
                for r in z_last(k, j):
                    r.wait_recv()
                total = total + decode(zr.at[k, j], zrs.at[k, j])
            encode(total / TOTAL, ec.at[k], ecs.at[k])
            owner, own_column, pairs, far = e_send(k)
            if own_column:
                @pl.when(owner == p)
                def _():
                    for i, (src, dst) in enumerate(pairs):
                        pltpu.make_async_copy(src, dst, erecv.at[i]).start()

                @pl.when(owner != p)
                def _():
                    for r in far:
                        r.start()
            else:
                for r in far:
                    r.start()

    def finish(k):
        @pl.when(z_place(k) == 2)
        def _():
            for r in z_halves(k):
                r.wait_send()

        @pl.when(z_place(k) % 2 == 1)
        def _():
            for r in z_last(k, 0):
                r.wait_send()

        owner, own_column, _, far = e_send(k)
        away = z_place(k) == 0
        if own_column:
            away = away & (owner != p)

        @pl.when(away)
        def _():
            for r in far:
                r.wait_send()

    forward(0, 0)
    head.wait_recv()
    for h in (0, 1):
        for j in range(NCH, NALL):
            to_y(0, h, j)
    forward(0, 1)
    gather(0, 0, FB)
    forward(0, 2)
    stage0(0)
    stage0(1)
    forward(0, 3)
    for j in range(NCH):
        to_y(0, 1, j)
        to_y(1, 1, j)
    stage1(0)
    from_z(0, 0)
    forward(0, 4)
    stage1(1)
    from_z(0, 1)
    forward(0, 5)
    stage2(0)
    stage2(1)
    forward(0, 6)
    forward(0, 7)
    coords1()
    for j in range(NCH):
        from_y(1, 0, j).wait_recv()
    stage0(2)
    forward(1, 6)
    forward(1, 7)
    stage0(3)
    stage3(0)
    stage3(1)
    forward(1, 0)
    stage1(2)
    stage1(3)
    coords2()
    forward(1, 1)
    following(0)
    gather(1, 0, HF)
    stage2(2)
    stage2(3)
    forward(1, 2)
    for j in range(2, NCH):
        from_z(0, j)
    stage0(4)
    stage4(0)
    stage4(1)
    forward(1, 3)
    centers1()
    stage1(4)
    for j in range(NCH, NALL):
        from_z(0, j)
    from_z(1, 0)
    from_z(1, 1)
    gather(3, 0, HF)
    forward(1, 4)
    stage3(2)
    stage3(3)
    stage2(4)
    forward(1, 5)
    stage5(0)
    stage5(1)
    centers2()
    for j in range(NCH):
        from_y(1, 1, j).wait_recv()

    def ready(k):
        if k == 7:
            following(1)
            gather(1, HF, HF)
        if k == 9:
            for j in range(2, NALL):
                from_z(1, j)
            gather(3, HF, HF)

    def run(stage, k):
        if 5 <= k < NU:
            stage(k)

    for step in range(5, NU + 9):
        if step < NU:
            ready(step)
            stage0(step)
        run(stage1, step - 1)
        run(stage2, step - 3)
        run(stage3, step - 5)
        run(stage4, step - 7)
        run(stage5, step - 9)
        if step == 5:
            stage3(4)
        if step == 6:
            stage4(2)
            stage4(3)
        if step == 8:
            stage4(4)
            centers3()
        if step == 9:
            stage5(2)
            stage5(3)
        if step == 11:
            stage5(4)
        if step == NU:
            nearest()

    pltpu.make_async_copy(oc, oc, erecv.at[0]).wait()
    pltpu.make_async_copy(ocs, ocs, erecv.at[1]).wait()
    for j in range(4):
        both_ref[pl.ds(j * XS, XS), :] = decode(oc.at[j], ocs.at[j])
    for r, cond in sent:
        if cond is None:
            r.wait_send()
        else:
            @pl.when(cond)
            def _(r=r):
                r.wait_send()
    for k in range(NU):
        finish(k)


def split(both_ref, coords_in, near_in, inst_ref, lag_ref, coords_ref, near_ref):
    inst_ref[...] = both_ref[:, 0:FB]
    lag_ref[...] = both_ref[:, FB:2 * FB]
    coords_ref[...] = coords_in[...]
    near_ref[...] = near_in[...].reshape(ROWS)


def per_device(frames_data, lag_index, projection, center_ids, nearest_prev):
    vmem = pl.BlockSpec(memory_space=pltpu.VMEM)
    dma = pltpu.SemaphoreType.DMA
    wide = 2 * FB
    both, coords, nearest = pl.pallas_call(
        kernel,
        out_shape=[
            jax.ShapeDtypeStruct((128, wide), F32),
            jax.ShapeDtypeStruct((K, ROWS), F32),
            jax.ShapeDtypeStruct((1, ROWS), F32),
        ],
        in_specs=[vmem] * 5,
        out_specs=[vmem] * 3,
        scratch_shapes=[
            pltpu.VMEM((4, FB, ROWS + LAG), BF16),
            pltpu.VMEM((3, FB, ROWS), BF16),
            pltpu.VMEM((NU, HF, wide), F32),
            pltpu.VMEM((NU, 128, wide), F32),
            pltpu.VMEM((NU, XS, wide), I16),
            pltpu.VMEM((NU, 1, wide), F32),
            pltpu.VMEM((NU, XS, wide), I16),
            pltpu.VMEM((NU, 2, 1, wide), F32),
            pltpu.VMEM((NU, 2, XS, wide), I16),
            pltpu.VMEM((NU, 2, 1, wide), F32),
            pltpu.VMEM((NU, 2, XS, wide), I16),
            pltpu.VMEM((NU, 2, 1, wide), F32),
            pltpu.VMEM((NU, XS, FB), I16),
            pltpu.VMEM((NU, 1, FB), F32),
            pltpu.VMEM((NU, XS, wide), I16),
            pltpu.VMEM((NU, 1, wide), F32),
            pltpu.VMEM((NU, 2, XS, wide), I16),
            pltpu.VMEM((NU, 2, 1, wide), F32),
            pltpu.VMEM((NU, XS, wide), F32),
            pltpu.VMEM((NU, XS, wide), I16),
            pltpu.VMEM((NU, 1, wide), F32),
            pltpu.VMEM((4, XS, wide), I16),
            pltpu.VMEM((4, 1, wide), F32),
            pltpu.VMEM((K, ROWS), F32),
            pltpu.VMEM((4, K // 4, ROWS), F32),
            pltpu.VMEM((2, K // 4, ROWS), F32),
            pltpu.VMEM((K, ROWS), F32),
            pltpu.VMEM((3, K // 4, C), F32),
            pltpu.VMEM((7, K // 4, C), F32),
            pltpu.VMEM((K, C), F32),
            dma((2, 2, NALL)), dma((2, 2, NALL)), dma((2, NALL)), dma((2, NALL)), dma((3, 2, 2)), dma(()),
            dma((NU,)), dma((NU,)), dma((NU, 2, 2)), dma((NU, 2, 2)), dma((NU, 2, 2)), dma((NU, 2, 2)),
            dma((NU, 2, 2)), dma((NU, 2)), dma((NU, 2)), dma((NU, 2, 2)), dma((NU, 2)), dma((2,)),
            dma((5,)), dma((5,)), dma((4,)), dma((4,)), dma((7,)), dma((7,)), dma((4,)), dma((4,)),
        ],
        compiler_params=pltpu.CompilerParams(collective_id=0, has_side_effects=True, vmem_limit_bytes=60 * 2**20),
        name="tica",
    )(
        frames_data,
        lag_index,
        projection.T,
        center_ids,
        nearest_prev,
    )
    return pl.pallas_call(
        split,
        out_shape=[
            jax.ShapeDtypeStruct((128, FB), F32),
            jax.ShapeDtypeStruct((128, FB), F32),
            jax.ShapeDtypeStruct((K, ROWS), F32),
            jax.ShapeDtypeStruct((ROWS,), F32),
        ],
        in_specs=[vmem] * 3,
        out_specs=[vmem] * 4,
        name="split",
    )(both, coords, nearest)


def solution(mesh):
    placed = (P("frames", "feats"), P("frames"), P("feats", None), P(), P("frames"))
    return jax.shard_map(
        per_device,
        mesh=mesh,
        in_specs=placed,
        out_specs=(P("frames", "feats"), P("frames", "feats"), P(None, "frames"), P("frames")),
        check_vma=False,
    )
```

profile of v0, /device:TPU:31, one launch (start us, length us, event | category | flops | bytes accessed | tf_op | source)
XLA Modules:
  0.0 129.6 jit_solution(977026557241377990)
XLA Ops:
  0.6 126.8 %tica.1 = (f32[128,1024]{1,0:T(8,128)}, f32[64,1536]{1,0:T(8,128)}, f32[1,1536]{1,0:T(1,128)}) custom-call(bf16[1536,512]{1,0:T(8,128)(2,1)} %x_ref.1, s32[1536]{0:T(1024)} %idx_ref.1, bf16[64,512]{1,0:T(8,128)(2,1)} %bitcast.1, s32[256]{0:T(256)} %ids_ref.1, f32[1536]{0:T(1024)} %prev_ref.1), custom_call_target="tpu_custom_call" | custom-call | tf_op jit(solution)/shard_map/tica/pallas_call | solution.py:519
  127.5 2.1 %split.1 = (f32[128,512]{1,0:T(8,128)}, f32[128,512]{1,0:T(8,128)}, f32[64,1536]{1,0:T(8,128)}, f32[1536]{0:T(1024)}) custom-call(f32[128,1024]{1,0:T(8,128)} %get-tuple-element.7.both_ref, f32[64,1536]{1,0:T(8,128)} %get-tuple-element.8.coords_in, f32[1,1536]{1,0:T(1,128)} %get-tuple-element.9.near_in), custom_call_target="tpu_custom_call" | custom-call | tf_op jit(solution)/shard_map/split/pallas_call | solution.py:573
where the time goes:
time: 130 us
  Pallas kernels  129 us (99%)
    pallas_call x1, Pallas kernels, per_device(): pl.pallas_call(kernel, out_shape=[jax.ShapeDtypeStruct((128, wide), F32),...  127 us

commit v1 on v0

--- a/solution.py
+++ b/solution.py
@@ -31,6 +31,7 @@
 )
 LAG_SLOT = {0: 0, 1: 1, 3: 2}
 NU = len(UNITS)
+DIRECT = 5
 XS = 32
 
 
@@ -159,17 +160,20 @@
             to_y(1, 0, j)
 
     kq = K // 4
-    cpart[...] = dot(proj_ref[...], xb[0, :, 0:ROWS], (1, 0))
-    crs = []
-    for t in (1, 3, 2):
-        rows = pl.ds(pl.multiple_of(((y + t) % 4) * kq, kq), kq)
-        crs.append(send(cpart.at[rows, :], crecv.at[t], psend.at[t], precv.at[t], yto(t)))
     for j in range(3, NCH):
         to_y(0, 0, j)
         to_y(1, 0, j)
     own_rows = pl.ds(pl.multiple_of(y * kq, kq), kq)
     first = p * ROWS
     small = {}
+
+    crs = []
+
+    def coords0():
+        cpart[...] = dot(proj_ref[...], xb[0, :, 0:ROWS], (1, 0))
+        for t in (1, 3, 2):
+            rows = pl.ds(pl.multiple_of(((y + t) % 4) * kq, kq), kq)
+            crs.append(send(cpart.at[rows, :], crecv.at[t], psend.at[t], precv.at[t], yto(t)))
 
     def coords1():
         for r in crs:
@@ -266,6 +270,16 @@
         u[k, mine, :] = u[k, mine, :] + cx[k]
         encode(u[k, slice_of((x + 2) % 4), :], s1.at[k], s1s.at[k])
         out = []
+        if k >= DIRECT:
+            for j, dev, xs in ((0, xp, (x + 1) % 4), (1, xm, (x + 3) % 4)):
+                encode(u[k, slice_of(xs), :], s2.at[k, j], s2s.at[k, j])
+                out.append(send(s2.at[k, j], r2.at[k, j], s2send.at[k, j, 0], s2recv.at[k, j, 0], dev))
+                out.append(send(s2s.at[k, j], r2s.at[k, j], s2send.at[k, j, 1], s2recv.at[k, j, 1], dev))
+            dev = (at(zh, (x + 2) % 4, c), q)
+            out.append(send(s1.at[k], r1.at[k], s1send.at[k, 0, 0], s1recv.at[k, 0, 0], dev))
+            out.append(send(s1s.at[k], r1s.at[k, 0], s1send.at[k, 0, 1], s1recv.at[k, 0, 1], dev))
+            s2w[k] = out
+            return
         for j, dev in ((0, xp), (1, xm)):
             rows = pl.ds(j * 16, 16)
             out.append(send(s1.at[k, rows, :], r1.at[k, rows, :], s1send.at[k, j, 0], s1recv.at[k, j, 0], dev))
@@ -273,6 +287,8 @@
         s1w[k] = out
 
     def stage2(k):
+        if k >= DIRECT:
+            return
         for r in s1w[k]:
             r.wait_recv()
         out = []
@@ -311,7 +327,18 @@
         for r in s2w[k]:
             r.wait_recv()
         rows = slice_of(x)
-        es[k] = u[k, rows, :] + decode(r2.at[k, 0], r2s.at[k, 0]) + decode(r2.at[k, 1], r2s.at[k, 1])
+        total = u[k, rows, :] + decode(r2.at[k, 0], r2s.at[k, 0]) + decode(r2.at[k, 1], r2s.at[k, 1])
+        if k >= DIRECT:
+            es[k] = total + decode(r1.at[k], r1s.at[k, 0])
+
+            @pl.when(z_place(k) != 0)
+            def _():
+                encode(es[k], zs.at[k], zss.at[k])
+                for r in z_last(k, z_place(k) - 1):
+                    r.start()
+
+            return
+        es[k] = total
 
         @pl.when(z_place(k) == 2)
         def _():
@@ -320,6 +347,8 @@
                 r.start()
 
     def stage4(k):
+        if k >= DIRECT:
+            return
         for j, place in ((0, 1), (1, 3)):
             @pl.when(z_place(k) == place)
             def _():
@@ -344,7 +373,7 @@
         @pl.when(z_place(k) == 0)
         def _():
             total = es[k]
-            for j in range(2):
+            for j in range(3 if k >= DIRECT else 2):
                 for r in z_last(k, j):
                     r.wait_recv()
                 total = total + decode(zr.at[k, j], zrs.at[k, j])
@@ -365,12 +394,13 @@
                     r.start()
 
     def finish(k):
-        @pl.when(z_place(k) == 2)
-        def _():
-            for r in z_halves(k):
-                r.wait_send()
-
-        @pl.when(z_place(k) % 2 == 1)
+        if k < DIRECT:
+            @pl.when(z_place(k) == 2)
+            def _():
+                for r in z_halves(k):
+                    r.wait_send()
+
+        @pl.when((z_place(k) != 0) if k >= DIRECT else (z_place(k) % 2 == 1))
         def _():
             for r in z_last(k, 0):
                 r.wait_send()
@@ -401,6 +431,7 @@
         to_y(1, 1, j)
     stage1(0)
     from_z(0, 0)
+    coords0()
     forward(0, 4)
     stage1(1)
     from_z(0, 1)
@@ -409,7 +440,6 @@
     stage2(1)
     forward(0, 6)
     forward(0, 7)
-    coords1()
     for j in range(NCH):
         from_y(1, 0, j).wait_recv()
     stage0(2)
@@ -421,7 +451,6 @@
     forward(1, 0)
     stage1(2)
     stage1(3)
-    coords2()
     forward(1, 1)
     following(0)
     gather(1, 0, HF)
@@ -434,7 +463,6 @@
     stage4(0)
     stage4(1)
     forward(1, 3)
-    centers1()
     stage1(4)
     for j in range(NCH, NALL):
         from_z(0, j)
@@ -448,7 +476,6 @@
     forward(1, 5)
     stage5(0)
     stage5(1)
-    centers2()
     for j in range(NCH):
         from_y(1, 1, j).wait_recv()
 
@@ -481,15 +508,23 @@
             stage4(3)
         if step == 8:
             stage4(4)
-            centers3()
         if step == 9:
             stage5(2)
             stage5(3)
         if step == 11:
             stage5(4)
-        if step == NU:
-            nearest()
-
+        if step == 6:
+            coords1()
+        if step == 8:
+            coords2()
+        if step == 10:
+            centers1()
+        if step == 12:
+            centers2()
+        if step == 14:
+            centers3()
+
+    nearest()
     pltpu.make_async_copy(oc, oc, erecv.at[0]).wait()
     pltpu.make_async_copy(ocs, ocs, erecv.at[1]).wait()
     for j in range(4):
@@ -542,8 +577,8 @@
             pltpu.VMEM((NU, 1, FB), F32),
             pltpu.VMEM((NU, XS, wide), I16),
             pltpu.VMEM((NU, 1, wide), F32),
-            pltpu.VMEM((NU, 2, XS, wide), I16),
-            pltpu.VMEM((NU, 2, 1, wide), F32),
+            pltpu.VMEM((NU, 3, XS, wide), I16),
+            pltpu.VMEM((NU, 3, 1, wide), F32),
             pltpu.VMEM((NU, XS, wide), F32),
             pltpu.VMEM((NU, XS, wide), I16),
             pltpu.VMEM((NU, 1, wide), F32),
@@ -558,7 +593,7 @@
             pltpu.VMEM((K, C), F32),
             dma((2, 2, NALL)), dma((2, 2, NALL)), dma((2, NALL)), dma((2, NALL)), dma((3, 2, 2)), dma(()),
             dma((NU,)), dma((NU,)), dma((NU, 2, 2)), dma((NU, 2, 2)), dma((NU, 2, 2)), dma((NU, 2, 2)),
-            dma((NU, 2, 2)), dma((NU, 2)), dma((NU, 2)), dma((NU, 2, 2)), dma((NU, 2)), dma((2,)),
+            dma((NU, 2, 2)), dma((NU, 2)), dma((NU, 2)), dma((NU, 3, 2)), dma((NU, 2)), dma((2,)),
             dma((5,)), dma((5,)), dma((4,)), dma((4,)), dma((7,)), dma((7,)), dma((4,)), dma((4,)),
         ],
         compiler_params=pltpu.CompilerParams(collective_id=0, has_side_effects=True, vmem_limit_bytes=60 * 2**20),

time: 130 us -> 128 us (0.985); the launches traced: 130 us -> 125 us
  Pallas kernels: 129 us -> 125 us
    pallas_call x1, Pallas kernels: 127 us -> 123 us  [per_device(): pl.pallas_call(kernel, out_shape=[jax.ShapeDtypeStruct((128, wide), F32),...]
where the time goes in v1:
time: 128 us; the launch traced here: 125 us
  Pallas kernels  125 us (98%)
    pallas_call x1, Pallas kernels, per_device(): pl.pallas_call(kernel, out_shape=[jax.ShapeDtypeStruct((128, wide), F32),...  123 us

profile of v1, /device:TPU:31, one launch (start us, length us, event | category | flops | bytes accessed | tf_op | source)
XLA Modules:
  0.0 125.4 jit_solution(11110898574632614500)
XLA Ops:
  0.6 122.7 %tica.1 = (f32[128,1024]{1,0:T(8,128)}, f32[64,1536]{1,0:T(8,128)}, f32[1,1536]{1,0:T(1,128)}) custom-call(bf16[1536,512]{1,0:T(8,128)(2,1)} %x_ref.1, s32[1536]{0:T(1024)} %idx_ref.1, bf16[64,512]{1,0:T(8,128)(2,1)} %bitcast.1, s32[256]{0:T(256)} %ids_ref.1, f32[1536]{0:T(1024)} %prev_ref.1), custom_call_target="tpu_custom_call" | custom-call | tf_op jit(solution)/shard_map/tica/pallas_call | solution.py:554
  123.3 2.1 %split.1 = (f32[128,512]{1,0:T(8,128)}, f32[128,512]{1,0:T(8,128)}, f32[64,1536]{1,0:T(8,128)}, f32[1536]{0:T(1024)}) custom-call(f32[128,1024]{1,0:T(8,128)} %get-tuple-element.7.both_ref, f32[64,1536]{1,0:T(8,128)} %get-tuple-element.8.coords_in, f32[1,1536]{1,0:T(1,128)} %get-tuple-element.9.near_in), custom_call_target="tpu_custom_call" | custom-call | tf_op jit(solution)/shard_map/split/pallas_call | solution.py:608

commit v2 on v1

--- a/solution.py
+++ b/solution.py
@@ -271,13 +271,13 @@
         encode(u[k, slice_of((x + 2) % 4), :], s1.at[k], s1s.at[k])
         out = []
         if k >= DIRECT:
+            dev = (at(zh, (x + 2) % 4, c), q)
+            out.append(send(s1.at[k], r1.at[k], s1send.at[k, 0, 0], s1recv.at[k, 0, 0], dev))
+            out.append(send(s1s.at[k], r1s.at[k, 0], s1send.at[k, 0, 1], s1recv.at[k, 0, 1], dev))
             for j, dev, xs in ((0, xp, (x + 1) % 4), (1, xm, (x + 3) % 4)):
                 encode(u[k, slice_of(xs), :], s2.at[k, j], s2s.at[k, j])
                 out.append(send(s2.at[k, j], r2.at[k, j], s2send.at[k, j, 0], s2recv.at[k, j, 0], dev))
                 out.append(send(s2s.at[k, j], r2s.at[k, j], s2send.at[k, j, 1], s2recv.at[k, j, 1], dev))
-            dev = (at(zh, (x + 2) % 4, c), q)
-            out.append(send(s1.at[k], r1.at[k], s1send.at[k, 0, 0], s1recv.at[k, 0, 0], dev))
-            out.append(send(s1s.at[k], r1s.at[k, 0], s1send.at[k, 0, 1], s1recv.at[k, 0, 1], dev))
             s2w[k] = out
             return
         for j, dev in ((0, xp), (1, xm)):

time: 128 us -> 128 us (level)
  no operation moved by 1% of the time
where the time goes in v2:
time: 128 us; the launch traced here: 126 us
  Pallas kernels  125 us (98%)
    pallas_call x1, Pallas kernels, per_device(): pl.pallas_call(kernel, out_shape=[jax.ShapeDtypeStruct((128, wide), F32),...  123 us

profile of v2, /device:TPU:31, one launch (start us, length us, event | category | flops | bytes accessed | tf_op | source)
XLA Modules:
  0.0 125.7 jit_solution(12607870788141657589)
XLA Ops:
  0.6 122.9 %tica.1 = (f32[128,1024]{1,0:T(8,128)}, f32[64,1536]{1,0:T(8,128)}, f32[1,1536]{1,0:T(1,128)}) custom-call(bf16[1536,512]{1,0:T(8,128)(2,1)} %x_ref.1, s32[1536]{0:T(1024)} %idx_ref.1, bf16[64,512]{1,0:T(8,128)(2,1)} %bitcast.1, s32[256]{0:T(256)} %ids_ref.1, f32[1536]{0:T(1024)} %prev_ref.1), custom_call_target="tpu_custom_call" | custom-call | tf_op jit(solution)/shard_map/tica/pallas_call | solution.py:554
  123.6 2.1 %split.1 = (f32[128,512]{1,0:T(8,128)}, f32[128,512]{1,0:T(8,128)}, f32[64,1536]{1,0:T(8,128)}, f32[1536]{0:T(1024)}) custom-call(f32[128,1024]{1,0:T(8,128)} %get-tuple-element.7.both_ref, f32[64,1536]{1,0:T(8,128)} %get-tuple-element.8.coords_in, f32[1,1536]{1,0:T(1,128)} %get-tuple-element.9.near_in), custom_call_target="tpu_custom_call" | custom-call | tf_op jit(solution)/shard_map/split/pallas_call | solution.py:608
